TPU v7x, 32 devices: a whole 2x2x4 slice. The times are simulated.
32 devices in a mesh: ctx: 8 (over z, core), tp: 4 (over y, x).
Axes of the slice: x: 2, y: 2, z: 4, core: 2. Of those that a mesh axis runs over, the one named last changes fastest.
Arguments:
- tokens: bfloat16 [2048, 2048], P(('ctx', 'tp')), may hold values from -16 to 16
- w_project: bfloat16 [2048, 12288], P(None, 'tp'), may hold values from -0.125 to 0.125
- w_mixers: bfloat16 [2048, 64], P(None, 'tp'), may hold values from -1 to 1
- conv_weight: bfloat16 [16, 4, 512], P('tp'), may hold values from -3 to 3
- decay_log: float32 [32], P('tp'), may hold values from 0 to 1
- step_bias: float32 [32], P('tp'), may hold values from -20 to -2
- norm_gain: float32 [128], replicated, may hold values from 0.1 to 1.9
- w_output: bfloat16 [4096, 2048], P('tp'), may hold values from -0.09375 to 0.09375
Outputs:
- mixed_rows: bfloat16 [2048, 2048], P(('ctx', 'tp'))
All inputs are finite; a program needn't handle non-finite values.
Results may differ from a plain program's by a relative error of at most 0.018.
Values may be sent and summed in bfloat16 or wider, within the bound.
A program may use at most 64 MiB of HBM per device.

v0:
```python
import jax
import jax.numpy as jnp
from jax import lax
from jax.sharding import PartitionSpec as P

SPAN = 64


EPSILON = 1e-06
TOP_PRECISION = lax.Precision.HIGHEST


def from_behind(value, axis, steps):
    count = lax.axis_size(axis)
    first, last = (max(0, -steps), min(count, count - steps))
    return lax.ppermute(value, axis, [(source, source + steps) for source in range(first, last)])


def unit_rows(values):
    values = values.astype(jnp.float32)
    return values * lax.rsqrt(jnp.sum(values * values, axis=-1, keepdims=True) + EPSILON)


def apply_map(map_part, add_part):
    return jnp.einsum("hij,hjk->hik", map_part, add_part, precision=TOP_PRECISION)


def on_device(tokens, w_project, w_mixers, conv_weight, decay_log, step_bias, norm_gain, w_output):
    gathered = lax.all_gather(tokens, "tp", axis=0, tiled=True)
    length = gathered.shape[0]
    key_heads = conv_weight.shape[0]
    conv_taps = conv_weight.shape[1]
    head_width = conv_weight.shape[2] // 4
    value_heads = 2 * key_heads
    projected = jnp.dot(gathered, w_project, preferred_element_type=jnp.float32).astype(
        jnp.bfloat16
    )
    projected = projected.reshape(length, key_heads, 6 * head_width)
    mixers = jnp.dot(gathered, w_mixers, preferred_element_type=jnp.float32).astype(jnp.bfloat16)
    mixers = mixers.reshape(length, key_heads, 4)
    conv_input = projected[:, :, : 4 * head_width]
    border = from_behind(conv_input[length - conv_taps + 1 :], "ctx", 1)
    extended = jnp.concatenate([border, conv_input], axis=0)
    summed = jnp.zeros((length, key_heads, 4 * head_width), jnp.float32)
    for offset in range(conv_taps):
        summed = summed + conv_weight[:, offset, :].astype(jnp.float32)[None] * extended[
            offset : offset + length
        ].astype(jnp.float32)
    activated = jax.nn.silu(summed).astype(jnp.bfloat16)
    query_rows = jnp.repeat(unit_rows(activated[:, :, :head_width]), 2, axis=1)
    key_columns = jnp.repeat(unit_rows(activated[:, :, head_width : 2 * head_width]), 2, axis=1)
    value_rows = (
        activated[:, :, 2 * head_width :]
        .astype(jnp.float32)
        .reshape(length, value_heads, head_width)
    )
    write_intensity = jax.nn.sigmoid(
        mixers[:, :, :2].astype(jnp.float32).reshape(length, value_heads)
    )
    decay_input = mixers[:, :, 2:].astype(jnp.float32).reshape(length, value_heads)
    log_decay = -jnp.exp(decay_log)[None, :] * jax.nn.softplus(decay_input + step_bias[None, :])
    blocks = length // SPAN

    def to_blocks(tensor):
        tensor = tensor.reshape((blocks, SPAN) + tensor.shape[1:])
        return jnp.moveaxis(tensor, 2, 0)

    query_blocks = to_blocks(query_rows)
    key_blocks = to_blocks(key_columns)
    vector_blocks = to_blocks(value_rows)
    strength_blocks = to_blocks(write_intensity)
    cumulative = jnp.cumsum(to_blocks(log_decay), axis=-1)
    position = jnp.arange(SPAN)
    inclusive = position[:, None] >= position[None, :]
    strict = position[:, None] > position[None, :]
    difference = cumulative[..., :, None] - cumulative[..., None, :]
    within = jnp.where(inclusive, jnp.exp(jnp.where(inclusive, difference, 0.0)), 0.0)
    keys_dot = jnp.einsum("hnck,hnsk->hncs", key_blocks, key_blocks, precision=TOP_PRECISION)
    lower_part = jnp.where(strict, strength_blocks[..., :, None] * within * keys_dot, 0.0)
    system = lower_part + jnp.eye(SPAN, dtype=jnp.float32)
    right_side = jnp.concatenate(
        [
            strength_blocks[..., None] * vector_blocks,
            (strength_blocks * jnp.exp(cumulative))[..., None] * key_blocks,
        ],
        axis=-1,
    )
    solved = jax.scipy.linalg.solve_triangular(system, right_side, lower=True, unit_diagonal=True)
    updates = solved[..., :head_width]
    corrector = solved[..., head_width:]
    span_total = cumulative[..., -1:]
    key_tail = jnp.exp(span_total - cumulative)[..., None] * key_blocks
    identity = jnp.eye(head_width, dtype=jnp.float32)
    transition = jnp.exp(span_total)[..., None] * identity - jnp.einsum(
        "hnsk,hnsj->hnkj", key_tail, corrector, precision=TOP_PRECISION
    )
    inject = jnp.einsum("hnsk,hnsv->hnkv", key_tail, updates, precision=TOP_PRECISION)
    scores = within * jnp.einsum(
        "hnck,hnsk->hncs", query_blocks, key_blocks, precision=TOP_PRECISION
    )
    query_reach = jnp.exp(cumulative)[..., None] * query_blocks - jnp.einsum(
        "hncs,hnsk->hnck", scores, corrector, precision=TOP_PRECISION
    )
    own_part = jnp.einsum("hncs,hnsv->hncv", scores, updates, precision=TOP_PRECISION)

    def advance(running, span_pair):
        map_before, add_before = running
        map_span, add_span = span_pair
        return (
            (apply_map(map_span, map_before), apply_map(map_span, add_before) + add_span),
            (map_before, add_before),
        )

    identity_maps = jnp.broadcast_to(identity, (value_heads, head_width, head_width))
    initial = (identity_maps, jnp.zeros((value_heads, head_width, head_width), jnp.float32))
    (map_device, add_device), (maps_before, adds_before) = lax.scan(
        advance, initial, (jnp.moveaxis(transition, 1, 0), jnp.moveaxis(inject, 1, 0))
    )
    maps_before = jnp.moveaxis(maps_before, 0, 1)
    adds_before = jnp.moveaxis(adds_before, 0, 1)
    local_out = own_part + jnp.einsum(
        "hnck,hnkv->hncv", query_reach, adds_before, precision=TOP_PRECISION
    )
    carry_map = jnp.einsum("hnck,hnkj->hncj", query_reach, maps_before, precision=TOP_PRECISION)
    chain_size = lax.axis_size("ctx")

    def relay_step(hop_index, relay_carry):
        outgoing, received = relay_carry
        received = from_behind(outgoing.astype(jnp.bfloat16), "ctx", 1).astype(outgoing.dtype)
        return (apply_map(map_device, received) + add_device, received)

    _, incoming = lax.fori_loop(
        0, chain_size - 1, relay_step, (add_device, jnp.zeros_like(add_device))
    )
    core_out = local_out + jnp.einsum(
        "hncj,hjv->hncv", carry_map, incoming, precision=TOP_PRECISION
    )
    core_low = lax.optimization_barrier(core_out.astype(jnp.bfloat16))
    widened = (
        jnp.moveaxis(core_low, 0, 2).reshape(length, value_heads, head_width).astype(jnp.float32)
    )
    gate_part = (
        projected[:, :, 4 * head_width :]
        .astype(jnp.float32)
        .reshape(length, value_heads, head_width)
    )
    scaled = widened * lax.rsqrt(jnp.mean(widened * widened, axis=-1, keepdims=True) + EPSILON)
    normed = (norm_gain * scaled * jax.nn.silu(gate_part)).astype(jnp.bfloat16)
    normed = normed.reshape(length, value_heads * head_width)
    return lax.psum_scatter(
        jnp.dot(normed, w_output, preferred_element_type=jnp.float32).astype(jnp.bfloat16),
        "tp",
        scatter_dimension=0,
        tiled=True,
    )


def solution(mesh):
    placed = (
        P(("ctx", "tp"), None),
        P(None, "tp"),
        P(None, "tp"),
        P("tp", None, None),
        P("tp"),
        P("tp"),
        P(),
        P("tp", None),
    )
    return jax.shard_map(
        on_device, mesh=mesh, in_specs=placed, out_specs=P(("ctx", "tp"), None), check_vma=False
    )
```

profile of v0, /device:TPU:24, one launch (start us, length us, event | category | flops | bytes accessed | tf_op | source)
XLA Modules:
  0.0 389.1 jit_solution(7877068857813886986)
XLA Ops:
  8.8 0.9 slice_convert_fusion.5
  9.7 27.1 %all-gather.2.cloned.1.call-done = bf16[256,2048]{1,0:T(8,128)(2,1)} async-done(((bf16[64,2048]{1,0:T(8,128)(2,1)}), bf16[256,2048]{1,0:T(8,128)(2,1)}) %all-gather.2.cloned.1.call-update) | async-done | bytes 1048592 | tf_op jit(solution)/shard_map/all_gather | solution.py:29
  36.8 1.6 convolution_convert_fusion.2
  38.5 9.5 %convolution_convert_fusion = bf16[256,3072]{1,0:T(8,128)(2,1)} fusion(bf16[256,2048]{1,0:T(8,128)(2,1)} %all-gather.2.cloned.1.call-done, bf16[2048,3072]{1,0:T(8,128)(2,1)} %param.13), kind=kOutput, calls=%fused_computation.15 | convolution fusion | flops 3222011904 | bytes 15204352 | tf_op jit(solution)/shard_map/dot_general | solution.py:35
  48.0 3.3 reshape.145
  51.5 2.1 collective-permute-start.1
  53.8 0.9 reduce_window_sum.11
  55.0 1.3 slice.81
  56.5 1.2 copy.72
  57.7 2.9 fusion.19
  62.3 0.8 copy.45
  63.5 1.1 broadcast_in_dim.32
  64.6 1.3 broadcast_multiply_fusion
  66.0 1.3 bitcast_multiply_fusion.1
  67.4 1.0 copy-done.1
  68.3 1.8 convolution_multiply_fusion.1
  70.1 2.8 fusion.27
  72.9 158.7 %custom-call.4 = f32[8,4,1,64,64]{3,4,2,1,0:T(8,128)} custom-call(f32[8,4,1,64,64]{4,3,2,1,0:T(8,128)} %fusion.27), custom_call_target="InvertDiagBlocksLowerTriangular" | custom-call | tf_op jit(solution)/shard_map/jit(_solve_triangular)/vmap(vmap())/triangular_solve | solution.py:88
  231.6 3.8 fusion.11
  235.4 2.2 fusion.39
  237.6 2.3 convolution_subtract_fusion
  239.9 5.1 %convolution_bitcast_fusion = f32[4,8,128,128]{3,2,0,1:T(8,128)} fusion(f32[8,4,64,256]{3,2,1,0:T(8,128)S(1)} %fusion.11, f32[8,4,64,128]{3,2,1,0:T(8,128)S(1)} %bitcast.125, f32[8,4,64]{2,1,0:T(4,128)S(1)} %copy.54), kind=kOutput, calls=%fused_computation.28 | convolution fusion | flops 402915328 | bytes 4210688 | tf_op jit(solution)/shard_map/hnsk,hnsv->hnkv/dot_general | solution.py:97
  245.0 5.6 %bitcast_subtract_fusion = f32[4,8,128,128]{3,2,0,1:T(8,128)} fusion(f32[128,128]{1,0:T(8,128)S(1)} %fusion.51, f32[4,8]{0,1:T(8,128)S(1)} %copy.53, f32[8,4,64,256]{3,2,1,0:T(8,128)S(1)} %fusion.11, f32[8,4,64,128]{3,2,1,0:T(8,128)S(1)} %bitcast.126, f32[8,4,64]{2,1,0:T(4,128)S(1)} %copy.54), kind=kOutput, calls=%fused_computation.22 | convolution fusion | flops 403963904 | bytes 4280320 | tf_op jit(solution)/shard_map/hnsk,hnsj->hnkj/dot_general | solution.py:94
  250.7 18.9 %while.30 = (s32[]{:T(128)}, f32[8,128,128]{2,1,0:T(8,128)S(1)}, f32[8,128,128]{2,1,0:T(8,128)S(1)}, f32[4,8,128,128]{3,2,1,0:T(8,128)}, f32[4,8,128,128]{3,2,1,...) while((s32[]{:T(128)}, f32[8,128,128]{2,1,0:T(8,128)S(1)}, ...), condition=%wide.region_4.5_spmd.clone, body=%wide.region_3.4_spmd.clone.sunk | while | flops 403046400 | bytes 7865975 | solution.py:116
  250.8 1.1 bitcast_dynamic-update-slice_fusion.3
  251.8 1.7 fusion.91
  253.5 1.9 convolution_add_fusion.6
  255.5 1.1 bitcast_dynamic-update-slice_fusion.3
  256.6 1.7 fusion.91
  258.3 1.9 convolution_add_fusion.6
  260.2 1.1 bitcast_dynamic-update-slice_fusion.3
  261.3 1.7 fusion.91
  263.0 1.9 convolution_add_fusion.6
  265.0 1.0 bitcast_dynamic-update-slice_fusion.3
  266.0 1.7 fusion.91
  267.7 1.9 convolution_add_fusion.6
  270.3 3.7 fusion.15
  274.0 3.1 fusion.20
  277.1 68.7 %while.29 = (s32[]{:T(128)}, bf16[8,128,128]{2,1,0:T(8,128)(2,1)}, f32[8,128,128]{2,1,0:T(8,128)}, f32[8,128,128]{2,1,0:T(8,128)S(1)}, f32[8,128,128]{2,1,0:T(8,128)S(1)}, /*index=5*/s32[]{:T(128)}) while((s32[]{:T(128)}, bf16[8,128,128]{2,1,0:T(8,128)(2,1)}, f32[8,128,128]{2,1,0:T(8,128)}, f32[8,128,128]{2,1,0:T(8,128)S(1)}, ...), condition=%wide.region_6.7_spmd, body=%wide.region_5.6_spmd.sunk | while | flops 201719808 | bytes 3407981 | solution.py:132
  277.1 2.0 collective-permute-start
  279.2 6.0 %collective-permute-done = bf16[8,128,128]{2,1,0:T(8,128)(2,1)S(1)} collective-permute-done((bf16[8,128,128]{2,1,0:T(8,128)(2,1)}, bf16[8,128,128]{2,1,0:T(8,128)(2,1)S(1)}, u32[]{:S(2)}, u32[]{:S(2)}) %collective-permute-start) | collective-permute-done | bytes 262176 | tf_op jit(solution)/shard_map/while/body/eval_jaxpr/ppermute | solution.py:16
  285.1 0.8 convert_element_type.191
  286.0 1.1 convolution_add_fusion.5
  287.1 1.9 collective-permute-start
  289.0 6.0 %collective-permute-done = bf16[8,128,128]{2,1,0:T(8,128)(2,1)S(1)} collective-permute-done((bf16[8,128,128]{2,1,0:T(8,128)(2,1)}, bf16[8,128,128]{2,1,0:T(8,128)(2,1)S(1)}, u32[]{:S(2)}, u32[]{:S(2)}) %collective-permute-start) | collective-permute-done | bytes 262176 | tf_op jit(solution)/shard_map/while/body/eval_jaxpr/ppermute | solution.py:16
  295.8 1.1 convolution_add_fusion.5
  296.9 1.9 collective-permute-start
  298.8 6.0 %collective-permute-done = bf16[8,128,128]{2,1,0:T(8,128)(2,1)S(1)} collective-permute-done((bf16[8,128,128]{2,1,0:T(8,128)(2,1)}, bf16[8,128,128]{2,1,0:T(8,128)(2,1)S(1)}, u32[]{:S(2)}, u32[]{:S(2)}) %collective-permute-start) | collective-permute-done | bytes 262176 | tf_op jit(solution)/shard_map/while/body/eval_jaxpr/ppermute | solution.py:16
  305.6 1.1 convolution_add_fusion.5
  306.7 1.9 collective-permute-start
  308.6 6.0 %collective-permute-done = bf16[8,128,128]{2,1,0:T(8,128)(2,1)S(1)} collective-permute-done((bf16[8,128,128]{2,1,0:T(8,128)(2,1)}, bf16[8,128,128]{2,1,0:T(8,128)(2,1)S(1)}, u32[]{:S(2)}, u32[]{:S(2)}) %collective-permute-start) | collective-permute-done | bytes 262176 | tf_op jit(solution)/shard_map/while/body/eval_jaxpr/ppermute | solution.py:16
  315.4 1.1 convolution_add_fusion.5
  316.5 1.9 collective-permute-start
  318.4 6.0 %collective-permute-done = bf16[8,128,128]{2,1,0:T(8,128)(2,1)S(1)} collective-permute-done((bf16[8,128,128]{2,1,0:T(8,128)(2,1)}, bf16[8,128,128]{2,1,0:T(8,128)(2,1)S(1)}, u32[]{:S(2)}, u32[]{:S(2)}) %collective-permute-start) | collective-permute-done | bytes 262176 | tf_op jit(solution)/shard_map/while/body/eval_jaxpr/ppermute | solution.py:16
  325.2 1.1 convolution_add_fusion.5
  326.3 1.9 collective-permute-start
  328.2 6.0 %collective-permute-done = bf16[8,128,128]{2,1,0:T(8,128)(2,1)S(1)} collective-permute-done((bf16[8,128,128]{2,1,0:T(8,128)(2,1)}, bf16[8,128,128]{2,1,0:T(8,128)(2,1)S(1)}, u32[]{:S(2)}, u32[]{:S(2)}) %collective-permute-start) | collective-permute-done | bytes 262176 | tf_op jit(solution)/shard_map/while/body/eval_jaxpr/ppermute | solution.py:16
  335.0 1.1 convolution_add_fusion.5
  336.1 1.9 collective-permute-start
  338.0 6.0 %collective-permute-done = bf16[8,128,128]{2,1,0:T(8,128)(2,1)S(1)} collective-permute-done((bf16[8,128,128]{2,1,0:T(8,128)(2,1)}, bf16[8,128,128]{2,1,0:T(8,128)(2,1)S(1)}, u32[]{:S(2)}, u32[]{:S(2)}) %collective-permute-start) | collective-permute-done | bytes 262176 | tf_op jit(solution)/shard_map/while/body/eval_jaxpr/ppermute | solution.py:16
  344.8 1.1 convolution_add_fusion.5
  345.9 2.1 fusion.28
  349.7 4.7 %convolution_convert_fusion.1 = bf16[256,2048]{1,0:T(8,128)(2,1)} fusion(bf16[1024,2048]{1,0:T(8,128)(2,1)} %param.19, f32[32,8,8,128]{3,2,1,0:T(8,128)S(1)} %bitcast.130, f32[32,8,8,128]{3,2,1,0:T(8,128)S(1)} %bitcast.132, f32[256,1024]{1,0:T(8,128)S(1)} %bitcast.131, f32[1024]{0:T(1024)S(1)} %broadcast_bitcast_fusion), kind=kOutput, calls=%fused_computation.16 | convolution fusion | flops 1076363264 | bytes 8392704 | tf_op jit(solution)/shard_map/dot_general | solution.py:151
  354.4 27.9 %reduce-scatter.2.cloned.1.call-done = bf16[64,2048]{1,0:T(8,128)(2,1)} async-done(((bf16[256,2048]{1,0:T(8,128)(2,1)}), bf16[64,2048]{1,0:T(8,128)(2,1)}) %reduce-scatter.2.cloned.1.call-update) | async-done | bytes 262160 | tf_op jit(solution)/shard_map/reduce_scatter | solution.py:150
  (85 shorter events, 12.8 us)
Async XLA Ops:
  6.5 30.3 %copy-start = (bf16[2048,16]{0,1:T(8,128)(2,1)S(1)}, bf16[2048,16]{0,1:T(8,128)(2,1)}, u32[]{:S(2)}) copy-start(bf16[2048,16]{0,1:T(8,128)(2,1)} %param.14) | copy-start | bytes 196612
  6.5 30.3 %all-gather.2.cloned.1.call-start = ((), (), s32[]{:S(2)}) async-start(), calls=%async_computation.1 | async-start | bytes 1310720 | tf_op jit(solution)/shard_map/all_gather | solution.py:29
  7.3 375.0 %reduce-scatter.2.cloned.1.call-start = ((), (), s32[]{:S(2)}) async-start(), calls=%async_computation.2 | async-start | bytes 1310720 | tf_op jit(solution)/shard_map/reduce_scatter | solution.py:150
  48.0 5.7 %copy-start.9 = (f32[8]{0:T(128)S(1)}, f32[8]{0:T(128)}, u32[]{:S(2)}) copy-start(f32[8]{0:T(128)} %param.17) | copy-start | bytes 100
  51.5 6.3 %collective-permute-start.1 = (bf16[3,4,512]{2,1,0:T(4,128)(2,1)S(1)}, bf16[3,4,512]{2,1,0:T(4,128)(2,1)S(1)}, u32[]{:S(2)}, u32[]{:S(2)}) collective-permute-start(bf16[3,4,512]{2,1,0:T(4,128)(2,1)S(1)} %slice.80), channel_id=1, source_target_pairs={{0,4},{4,8},{8,12},{12,16},{16,20},{20,24},{24,28},{1,5},{5,9},{9,... | collective-permute-start | bytes 36872 | tf_op jit(solution)/shard_map/ppermute | solution.py:16
  56.3 1.4 copy-start.6
  67.4 1.0 copy-start.1
  235.4 2.2 copy-start.2
  250.6 19.7 %copy-start.3 = (f32[8,4,64,128]{3,2,1,0:T(8,128)S(1)}, f32[8,4,64,128]{3,2,1,0:T(8,128)}, u32[]{:S(2)}) copy-start(f32[8,4,64,128]{3,2,1,0:T(8,128)} %convolution_subtract_fusion) | copy-start | bytes 3145732
  270.3 3.7 copy-start.4
  270.3 3.7 copy-start.7
  277.1 68.8 %copy-start.5 = (f32[8,4,64,128]{3,2,1,0:T(8,128)S(1)}, f32[8,4,64,128]{3,2,1,0:T(8,128)}, u32[]{:S(2)}) copy-start(f32[8,4,64,128]{3,2,1,0:T(8,128)} %fusion.20) | copy-start | bytes 3145732
  277.1 8.0 %collective-permute-start = (bf16[8,128,128]{2,1,0:T(8,128)(2,1)}, bf16[8,128,128]{2,1,0:T(8,128)(2,1)S(1)}, u32[]{:S(2)}, u32[]{:S(2)}) collective-permute-start(bf16[8,128,128]{2,1,0:T(8,128)(2,1)} %get-tuple-element.278), channel_id=1, source_target_pairs={{0,4},{4,8},{8,12},{12,16},{16,20},{20,24},{24,28},{1,5},{5,9},{9,... | collective-permute-start | bytes 786440 | tf_op jit(solution)/shard_map/while/body/eval_jaxpr/ppermute | solution.py:16
  287.1 7.9 %collective-permute-start = (bf16[8,128,128]{2,1,0:T(8,128)(2,1)}, bf16[8,128,128]{2,1,0:T(8,128)(2,1)S(1)}, u32[]{:S(2)}, u32[]{:S(2)}) collective-permute-start(bf16[8,128,128]{2,1,0:T(8,128)(2,1)} %get-tuple-element.278), channel_id=1, source_target_pairs={{0,4},{4,8},{8,12},{12,16},{16,20},{20,24},{24,28},{1,5},{5,9},{9,... | collective-permute-start | bytes 786440 | tf_op jit(solution)/shard_map/while/body/eval_jaxpr/ppermute | solution.py:16
  296.9 7.9 %collective-permute-start = (bf16[8,128,128]{2,1,0:T(8,128)(2,1)}, bf16[8,128,128]{2,1,0:T(8,128)(2,1)S(1)}, u32[]{:S(2)}, u32[]{:S(2)}) collective-permute-start(bf16[8,128,128]{2,1,0:T(8,128)(2,1)} %get-tuple-element.278), channel_id=1, source_target_pairs={{0,4},{4,8},{8,12},{12,16},{16,20},{20,24},{24,28},{1,5},{5,9},{9,... | collective-permute-start | bytes 786440 | tf_op jit(solution)/shard_map/while/body/eval_jaxpr/ppermute | solution.py:16
  306.7 7.9 %collective-permute-start = (bf16[8,128,128]{2,1,0:T(8,128)(2,1)}, bf16[8,128,128]{2,1,0:T(8,128)(2,1)S(1)}, u32[]{:S(2)}, u32[]{:S(2)}) collective-permute-start(bf16[8,128,128]{2,1,0:T(8,128)(2,1)} %get-tuple-element.278), channel_id=1, source_target_pairs={{0,4},{4,8},{8,12},{12,16},{16,20},{20,24},{24,28},{1,5},{5,9},{9,... | collective-permute-start | bytes 786440 | tf_op jit(solution)/shard_map/while/body/eval_jaxpr/ppermute | solution.py:16
  316.5 7.9 %collective-permute-start = (bf16[8,128,128]{2,1,0:T(8,128)(2,1)}, bf16[8,128,128]{2,1,0:T(8,128)(2,1)S(1)}, u32[]{:S(2)}, u32[]{:S(2)}) collective-permute-start(bf16[8,128,128]{2,1,0:T(8,128)(2,1)} %get-tuple-element.278), channel_id=1, source_target_pairs={{0,4},{4,8},{8,12},{12,16},{16,20},{20,24},{24,28},{1,5},{5,9},{9,... | collective-permute-start | bytes 786440 | tf_op jit(solution)/shard_map/while/body/eval_jaxpr/ppermute | solution.py:16
  326.3 7.9 %collective-permute-start = (bf16[8,128,128]{2,1,0:T(8,128)(2,1)}, bf16[8,128,128]{2,1,0:T(8,128)(2,1)S(1)}, u32[]{:S(2)}, u32[]{:S(2)}) collective-permute-start(bf16[8,128,128]{2,1,0:T(8,128)(2,1)} %get-tuple-element.278), channel_id=1, source_target_pairs={{0,4},{4,8},{8,12},{12,16},{16,20},{20,24},{24,28},{1,5},{5,9},{9,... | collective-permute-start | bytes 786440 | tf_op jit(solution)/shard_map/while/body/eval_jaxpr/ppermute | solution.py:16
  336.1 7.9 %collective-permute-start = (bf16[8,128,128]{2,1,0:T(8,128)(2,1)}, bf16[8,128,128]{2,1,0:T(8,128)(2,1)S(1)}, u32[]{:S(2)}, u32[]{:S(2)}) collective-permute-start(bf16[8,128,128]{2,1,0:T(8,128)(2,1)} %get-tuple-element.278), channel_id=1, source_target_pairs={{0,4},{4,8},{8,12},{12,16},{16,20},{20,24},{24,28},{1,5},{5,9},{9,... | collective-permute-start | bytes 786440 | tf_op jit(solution)/shard_map/while/body/eval_jaxpr/ppermute | solution.py:16
  348.5 1.2 copy-start.8
Sparse Core Ops, SparseCore 0:
  9.2 27.5 all-gather.1
  354.5 27.7 reduce-scatter.1
where the time goes:
time: 392 us; the launch traced here: 389 us
  other arithmetic  180 us (46%)
  waiting for transfers between devices  97.5 us (25%)
  matrix products  70 us (18%)
  starting transfers between devices  15.6 us (4%)
  between operations  13.8 us (4%)
  local copies, waits for them, and re-layouts  12 us (3%)
    another operation x3, other arithmetic, on_device(): jax.scipy.linalg.solve_triangular(system, right_side, lower=True, unit_di...  159 us
    ppermute x8, waiting for transfers between devices, from_behind(): lax.ppermute(value, axis, [(source, source + steps) for source in range(f...  41.8 us
    reduce_scatter x1, waiting for transfers between devices, on_device(): lax.psum_scatter(jnp.dot(normed, w_output, preferred_element_type=jnp.flo...  27.9 us
    all_gather x1, waiting for transfers between devices, on_device(): gathered = lax.all_gather(tokens, 'tp', axis=0, tiled=True)  27.1 us
    dot_general x15, matrix products, apply_map(): jnp.einsum('hij,hjk->hik', map_part, add_part, precision=TOP_PRECISION)  21.7 us
    ppermute x8, starting transfers between devices, from_behind(): lax.ppermute(value, axis, [(source, source + steps) for source in range(f...  15.6 us
    dot_general x1, matrix products, on_device(): jnp.dot(gathered, w_project, preferred_element_type=jnp.float32)  9.51 us
  transfers between devices with their start and end apart: 10, of which 9 were waited for; matrix products, arithmetic and copies ran while one was open for 2% of the time, Pallas kernels for 0%

commit v1 on v0

v1 whole, which is shorter than its diff:
```python
import functools

import jax
import jax.numpy as jnp
from jax import lax
from jax.experimental import pallas as pl
from jax.experimental.pallas import tpu as pltpu
from jax.sharding import PartitionSpec as P

EPSILON = 1e-06
TOP_PRECISION = lax.Precision.HIGHEST
MESH = pl.DeviceIdType.MESH
WIDTH = 128
F32 = jnp.float32
BF16 = jnp.bfloat16
BORDER = 16
LEAST_LOG = -120.0


def mm(a, b):
    return jnp.dot(a, b, preferred_element_type=F32)


def mm_rows(a, b):
    return lax.dot_general(a, b, (((1,), (1,)), ((), ())), preferred_element_type=F32)


def mm_over_rows(a, b):
    return lax.dot_general(a, b, (((0,), (0,)), ((), ())), preferred_element_type=F32)


def sigmoid(x):
    return 1.0 / (1.0 + jnp.exp(-x))


def softplus(x):
    small = jnp.exp(-jnp.abs(x))
    grown = 1.0 + small
    tail = jnp.where(grown == 1.0, small, jnp.log(grown) * small / jnp.where(grown == 1.0, 1.0, grown - 1.0))
    return jnp.maximum(x, 0.0) + tail


def kernel(
    n_ctx, n_tp, key_heads, batch,
    tok_ref, wp_ref, wm_ref, cw_ref, dl_ref, sb_ref, gain_ref, wo_ref,
    out_ref,
    gath, wp, wm, wo, ext, gate, act, border_out, border_in, col, row, minus, inject, own, reach,
    s_in, s_out, decay_all, normed, stage, landed,
    own_sem, wp_sem, wm_sem, wo_sem, ag_send, ag_recv, border_sem, state_send, state_recv, rs_send, rs_recv,
):
    rows = tok_ref.shape[0]
    length = rows * n_tp
    heads = 2 * key_heads
    depth = wo_ref.shape[1]
    ctx, tp = lax.axis_index("ctx"), lax.axis_index("tp")
    six, four = 6 * WIDTH, 4 * WIDTH

    wm_copy = pltpu.make_async_copy(wm_ref, wm, wm_sem)
    wo_copy = pltpu.make_async_copy(wo_ref, wo, wo_sem)
    wp_copies = [
        pltpu.make_async_copy(wp_ref.at[:, pl.ds(g * six, six)], wp.at[g], wp_sem.at[g]) for g in range(key_heads)
    ]
    mine = pl.ds(pl.multiple_of(tp * rows, 16), rows)
    own_copy = pltpu.make_async_copy(tok_ref, gath.at[mine], own_sem)
    own_copy.start()
    for copy in wp_copies:
        copy.start()
    wm_copy.start()
    wo_copy.start()

    barrier = pltpu.get_barrier_semaphore()
    peers = [lax.rem(tp + k, n_tp) for k in range(1, n_tp)]
    for peer in peers:
        pl.semaphore_signal(barrier, inc=1, device_id={"tp": peer}, device_id_type=MESH)

    @pl.when(ctx > 0)
    def _():
        pl.semaphore_signal(barrier, inc=1, device_id={"ctx": ctx - 1}, device_id_type=MESH)

    @pl.when(ctx < n_ctx - 1)
    def _():
        pl.semaphore_signal(barrier, inc=1, device_id={"ctx": ctx + 1}, device_id_type=MESH)

    beside = jnp.where(ctx > 0, 1, 0) + jnp.where(ctx < n_ctx - 1, 1, 0)
    pl.semaphore_wait(barrier, n_tp - 1 + beside)

    gathers = [
        pltpu.make_async_remote_copy(
            src_ref=tok_ref, dst_ref=gath.at[mine], send_sem=ag_send.at[k], recv_sem=ag_recv.at[k],
            device_id={"tp": peer}, device_id_type=MESH,
        )
        for k, peer in enumerate(peers)
    ]
    for copy in gathers:
        copy.start()

    own_copy.wait()
    wm_copy.wait()
    for copy in wp_copies:
        copy.wait()
    for copy in gathers:
        copy.wait()

    def project(g, carry):
        for t in range(2):
            part = mm(gath[...], wp[g, :, t * 256 : (t + 1) * 256]).astype(BF16)
            ext[8 : 8 + length, pl.ds(pl.multiple_of(g * four + t * 256, 256), 256)] = part.astype(F32)
        return carry

    lax.fori_loop(0, key_heads, project, 0)

    border_out[...] = ext[8 + length - BORDER : 8 + length, :].astype(BF16)
    border_copy = pltpu.make_async_remote_copy(
        src_ref=border_out, dst_ref=border_in, send_sem=border_sem.at[0], recv_sem=border_sem.at[1],
        device_id={"ctx": lax.rem(ctx + 1, n_ctx)}, device_id_type=MESH,
    )

    @pl.when(ctx < n_ctx - 1)
    def _():
        border_copy.start()

    def project_gate(g, carry):
        part = mm(gath[...], wp[g, :, four:six]).astype(BF16)
        gate[:, pl.ds(pl.multiple_of(g * 256, 256), 256)] = part
        return carry

    lax.fori_loop(0, key_heads, project_gate, 0)

    mixers = mm(gath[...], wm[...]).astype(BF16).astype(F32)
    columns = mixers.shape[1]
    lane = lax.broadcasted_iota(jnp.int32, (1, columns), 1)
    rate = jnp.zeros((1, columns), F32)
    bias = jnp.zeros((1, columns), F32)
    for h in range(heads):
        here = lane == 4 * (h // 2) + 2 + h % 2
        rate = jnp.where(here, dl_ref[0, h], rate)
        bias = jnp.where(here, sb_ref[0, h], bias)
    strength = sigmoid(mixers)
    log_decay = jnp.maximum(-jnp.exp(rate) * softplus(mixers + bias), LEAST_LOG)
    at_row = lax.broadcasted_iota(jnp.int32, (length, length), 0)
    at_col = lax.broadcasted_iota(jnp.int32, (length, length), 1)
    lower = jnp.where(at_row >= at_col, 1.0, 0.0)
    cumulative = jnp.dot(lower, log_decay, precision=TOP_PRECISION, preferred_element_type=F32)

    @pl.when(ctx > 0)
    def _():
        border_copy.wait_recv()
        ext[0:8, :] = border_in[BORDER - 8 : BORDER, :].astype(F32)

    @pl.when(ctx == 0)
    def _():
        ext[0:8, :] = jnp.zeros((8, ext.shape[1]), F32)

    def convolve(g, carry):
        for t in range(4):
            place = pl.ds(pl.multiple_of(g * four + t * WIDTH, WIDTH), WIDTH)
            taps = cw_ref[g, :, t * WIDTH : (t + 1) * WIDTH].astype(F32)
            total = taps[0:1] * ext[5 : 5 + length, place]
            for j in range(1, 4):
                total = total + taps[j : j + 1] * ext[5 + j : 5 + j + length, place]
            act[:, place] = (total * sigmoid(total)).astype(BF16)
        return carry

    lax.fori_loop(0, key_heads, convolve, 0)

    wide = lax.broadcasted_iota(jnp.int32, (length, WIDTH), 1)
    for g in range(key_heads):
        query = act[:, g * four : g * four + WIDTH].astype(F32)
        key = act[:, g * four + WIDTH : g * four + 2 * WIDTH].astype(F32)
        query_unit = lax.rsqrt(jnp.sum(query * query, axis=1, keepdims=True) + EPSILON)
        key_unit = lax.rsqrt(jnp.sum(key * key, axis=1, keepdims=True) + EPSILON)
        for r in range(2):
            h = 2 * g + r
            cum = cumulative[:, 4 * g + 2 + r : 4 * g + 3 + r]
            beta = strength[:, 4 * g + r : 4 * g + r + 1]
            packed = jnp.where(
                wide == 0, cum, jnp.where(wide == 1, beta, jnp.where(wide == 2, key_unit, query_unit))
            )
            col[h] = packed
            row[h] = jnp.transpose(packed)[0:8]

    def heads_of(step, carry):
        i = lax.broadcasted_iota(jnp.int32, (length, length), 0)
        j = lax.broadcasted_iota(jnp.int32, (length, length), 1)
        apart = jnp.bitwise_xor(i, j)
        lows, inverses, scored = [], [], []
        for b in range(batch):
            g = step * batch + b
            query = act[:, pl.ds(pl.multiple_of(g * four, WIDTH), WIDTH)]
            key = act[:, pl.ds(pl.multiple_of(g * four + WIDTH, WIDTH), WIDTH)]
            key_key = mm_rows(key, key)
            query_key = mm_rows(query, key)
            for r in range(2):
                h = 2 * g + r
                scal, across = col[h], row[h]
                cum, beta, key_unit, query_unit = (scal[:, n : n + 1] for n in range(4))
                within = jnp.where(i >= j, jnp.exp(jnp.where(i >= j, cum - across[0:1], 0.0)), 0.0) * across[2:3]
                scored.append((within * query_key * query_unit).astype(BF16))
                low = jnp.where(i > j, within * key_key * (beta * key_unit), 0.0).astype(BF16)
                lows.append(low)
                inverses.append(jnp.where(i == j, 1.0, jnp.where(apart == 1, -low.astype(F32), 0.0)).astype(BF16))
        span = 2
        while span < length:
            between = (apart >= span) & (apart < 2 * span)
            firsts = [
                mm(t, jnp.where(between, low.astype(F32), 0.0).astype(BF16)).astype(BF16)
                for t, low in zip(inverses, lows)
            ]
            inverses = [t - mm(first, t).astype(BF16) for t, first in zip(inverses, firsts)]
            span *= 2
        for n, (inverse, scores) in enumerate(zip(inverses, scored)):
            g = step * batch + n // 2
            r = n % 2
            h = 2 * g + r
            scal = col[h]
            cum, beta, key_unit, query_unit = (scal[:, m : m + 1] for m in range(4))
            query = act[:, pl.ds(pl.multiple_of(g * four, WIDTH), WIDTH)].astype(F32)
            key = act[:, pl.ds(pl.multiple_of(g * four + WIDTH, WIDTH), WIDTH)].astype(F32)
            vector = act[:, pl.ds(pl.multiple_of(g * four + (2 + r) * WIDTH, WIDTH), WIDTH)].astype(F32)
            reached = jnp.exp(cum)
            last = cum[length - 1 : length]
            right = jnp.concatenate([vector * beta, key * (beta * reached * key_unit)], axis=1).astype(BF16)
            solved = mm(inverse, right).astype(BF16)
            tail = (key * (jnp.exp(last - cum) * key_unit)).astype(BF16)
            ends = mm_over_rows(tail, solved)
            inject[h] = ends[:, :WIDTH]
            minus[h] = ends[:, WIDTH:].astype(BF16)
            decay_all[h] = jnp.broadcast_to(jnp.exp(last), (8, WIDTH))
            local = mm(scores, solved)
            own[h] = local[:, :WIDTH]
            reach[h] = (query * (reached * query_unit) - local[:, WIDTH:]).astype(BF16)
        return carry

    lax.fori_loop(0, key_heads // batch, heads_of, 0)

    def state_copy(h):
        return pltpu.make_async_remote_copy(
            src_ref=s_out.at[h], dst_ref=s_in.at[h], send_sem=state_send.at[h], recv_sem=state_recv.at[h],
            device_id={"ctx": lax.rem(ctx + 1, n_ctx)}, device_id_type=MESH,
        )

    for h in range(heads):
        @pl.when(ctx > 0)
        def _():
            state_copy(h).wait_recv()
            before = s_in[h]
            after = decay_all[h, 0:1, :] * before.astype(F32) - mm(minus[h], before) + inject[h]
            s_out[h] = after.astype(BF16)

        @pl.when(ctx == 0)
        def _():
            s_in[h] = jnp.zeros((WIDTH, WIDTH), BF16)
            s_out[h] = inject[h].astype(BF16)

        @pl.when(ctx < n_ctx - 1)
        def _():
            state_copy(h).start()

    def finish(h, carry):
        core = (own[h] + mm(reach[h], s_in[h])).astype(BF16).astype(F32)
        place = pl.ds(pl.multiple_of(h * WIDTH, WIDTH), WIDTH)
        gated = gate[:, place].astype(F32)
        scaled = core * lax.rsqrt(jnp.mean(core * core, axis=1, keepdims=True) + EPSILON)
        normed[:, place] = (gain_ref[...] * scaled * (gated * sigmoid(gated))).astype(BF16)
        return carry

    lax.fori_loop(0, heads, finish, 0)

    wo_copy.wait()
    pieces = rs_send.shape[0]
    piece = depth // pieces

    def share_copy(q, k):
        peer = lax.rem(tp + k + 1, n_tp)
        place = pl.ds(q * piece, piece)
        return pltpu.make_async_remote_copy(
            src_ref=stage.at[pl.ds(pl.multiple_of(peer * rows, 16), rows), place],
            dst_ref=landed.at[k, :, place],
            send_sem=rs_send.at[q, k], recv_sem=rs_recv.at[q, k],
            device_id={"tp": peer}, device_id_type=MESH,
        )

    for q in range(pieces):
        for t in range(0, piece, 256):
            place = slice(q * piece + t, q * piece + t + 256)
            stage[:, place] = mm(normed[...], wo[:, place]).astype(BF16)
        for k in range(n_tp - 1):
            share_copy(q, k).start()
    for q in range(pieces):
        place = slice(q * piece, (q + 1) * piece)
        total = stage[mine, place].astype(F32)
        for k in range(n_tp - 1):
            share_copy(q, k).wait_recv()
            total = total + landed[k, :, place].astype(F32)
        out_ref[:, place] = total.astype(BF16)
    for q in range(pieces):
        for k in range(n_tp - 1):
            share_copy(q, k).wait_send()

    @pl.when(ctx < n_ctx - 1)
    def _():
        border_copy.wait_send()
        for h in range(heads):
            state_copy(h).wait_send()


def on_device(tokens, w_project, w_mixers, conv_weight, decay_log, step_bias, norm_gain, w_output):
    n_ctx, n_tp = lax.axis_size("ctx"), lax.axis_size("tp")
    rows, depth = tokens.shape
    length = rows * n_tp
    key_heads = conv_weight.shape[0]
    heads = 2 * key_heads
    inner = heads * WIDTH
    batch = 2 if key_heads % 2 == 0 else 1
    pieces = 4
    vmem = pl.BlockSpec(memory_space=pltpu.VMEM)
    smem = pl.BlockSpec(memory_space=pltpu.SMEM)
    far = pl.BlockSpec(memory_space=pl.ANY)
    dma = pltpu.SemaphoreType.DMA
    square = (heads, WIDTH, WIDTH)
    return pl.pallas_call(
        functools.partial(kernel, n_ctx, n_tp, key_heads, batch),
        out_shape=jax.ShapeDtypeStruct((rows, depth), BF16),
        in_specs=[far, far, far, vmem, smem, smem, vmem, far],
        out_specs=vmem,
        scratch_shapes=[
            pltpu.VMEM((length, depth), BF16),
            pltpu.VMEM((key_heads, depth, 6 * WIDTH), BF16),
            pltpu.VMEM(w_mixers.shape, BF16),
            pltpu.VMEM(w_output.shape, BF16),
            pltpu.VMEM((8 + length, key_heads * 4 * WIDTH), F32),
            pltpu.VMEM((length, inner), BF16),
            pltpu.VMEM((length, key_heads * 4 * WIDTH), BF16),
            pltpu.VMEM((BORDER, key_heads * 4 * WIDTH), BF16),
            pltpu.VMEM((BORDER, key_heads * 4 * WIDTH), BF16),
            pltpu.VMEM((heads, length, WIDTH), F32),
            pltpu.VMEM((heads, 8, length), F32),
            pltpu.VMEM(square, BF16),
            pltpu.VMEM(square, F32),
            pltpu.VMEM((heads, length, WIDTH), F32),
            pltpu.VMEM((heads, length, WIDTH), BF16),
            pltpu.VMEM(square, BF16),
            pltpu.VMEM(square, BF16),
            pltpu.VMEM((heads, 8, WIDTH), F32),
            pltpu.VMEM((length, inner), BF16),
            pltpu.VMEM((length, depth), BF16),
            pltpu.VMEM((n_tp - 1, rows, depth), BF16),
            dma, dma((key_heads,)), dma, dma,
            dma((n_tp - 1,)), dma((n_tp - 1,)), dma((2,)),
            dma((heads,)), dma((heads,)),
            dma((pieces, n_tp - 1)), dma((pieces, n_tp - 1)),
        ],
        compiler_params=pltpu.CompilerParams(
            collective_id=0, has_side_effects=True, vmem_limit_bytes=52 * 1024 * 1024
        ),
    )(
        tokens, w_project, w_mixers, conv_weight,
        decay_log.reshape(1, heads), step_bias.reshape(1, heads), norm_gain.reshape(1, WIDTH), w_output,
    )


def solution(mesh):
    placed = (
        P(("ctx", "tp"), None),
        P(None, "tp"),
        P(None, "tp"),
        P("tp", None, None),
        P("tp"),
        P("tp"),
        P(),
        P("tp", None),
    )
    return jax.shard_map(
        on_device, mesh=mesh, in_specs=placed, out_specs=P(("ctx", "tp"), None), check_vma=False
    )
```

time: 392 us -> 67.2 us (0.17)
  other arithmetic: 180 us -> 0 us
  waiting for transfers between devices: 97.5 us -> 0 us
  matrix products: 70 us -> 0 us
  Pallas kernels: 0 us -> 60.8 us
  starting transfers between devices: 15.6 us -> 0 us
  between operations: 13.8 us -> 0.03 us
  local copies, waits for them, and re-layouts: 12 us -> 5.44 us
    another operation x7 -> x0, other arithmetic: 160 us -> none  [the longest x3 159 us: on_device(): jax.scipy.linalg.solve_triangular(system, right_side, lower=True, unit_di...]
    dot_general x27 -> x0, matrix products: 66.2 us -> none  [the longest x15 21.7 us: apply_map(): jnp.einsum('hij,hjk->hik', map_part, add_part, precision=TOP_PRECISION)]
    pallas_call x0 -> x1, Pallas kernels: none -> 60.8 us  [on_device(): pl.pallas_call(functools.partial(kernel, n_ctx, n_tp, key_heads, batch),...]
    ppermute x8 -> x0, waiting for transfers between devices: 41.8 us -> none  [from_behind(): lax.ppermute(value, axis, [(source, source + steps) for source in range(f...]
    reduce_scatter x1 -> x0, waiting for transfers between devices: 27.9 us -> none  [on_device(): lax.psum_scatter(jnp.dot(normed, w_output, preferred_element_type=jnp.flo...]
    all_gather x1 -> x0, waiting for transfers between devices: 27.1 us -> none  [on_device(): gathered = lax.all_gather(tokens, 'tp', axis=0, tiled=True)]
    ppermute x8 -> x0, starting transfers between devices: 15.6 us -> none  [from_behind(): lax.ppermute(value, axis, [(source, source + steps) for source in range(f...]
    convert_element_type x11 -> x0, other arithmetic: 9.74 us -> none  [the longest x7 5.8 us: relay_step(): from_behind(outgoing.astype(jnp.bfloat16), 'ctx', 1).astype(outgoing.dtype)]
  transfers between devices with their start and end apart: 10 -> 0, of which waited for: 9 -> 0; matrix products, arithmetic and copies ran while one was open for 2% -> 0% of each run, Pallas kernels for 0% -> 0%
where the time goes in v1:
time: 67.2 us; the launch traced here: 66.3 us
  Pallas kernels  60.8 us (90%)
  local copies, waits for them, and re-layouts  5.44 us (8%)
    pallas_call x1, Pallas kernels, on_device(): pl.pallas_call(functools.partial(kernel, n_ctx, n_tp, key_heads, batch),...  60.8 us
    unnamed x12, local copies, waits for them, and re-layouts  5.44 us

profile of v1, /device:TPU:24, one launch (start us, length us, event | category | flops | bytes accessed | tf_op | source)
XLA Modules:
  0.0 66.3 jit_solution(6219933905868245321)
XLA Ops:
  0.0 1.1 %copy.9.wm_ref = bf16[2048,16]{1,0:T(8,128)(2,1)S(1)} copy(bf16[2048,16]{0,1:T(8,128)(2,1)} %param.10) | data formatting | bytes 131072 | tf_op args[2]
  1.1 0.0 copy-start
  1.1 0.9 %copy-done = bf16[64,2048]{1,0:T(8,128)(2,1)S(1)} copy-done((bf16[64,2048]{1,0:T(8,128)(2,1)S(1)}, bf16[64,2048]{1,0:T(8,128)(2,1)}, u32[]{:S(2)}) %copy-start) | copy-done | bytes 262168
  2.1 0.0 copy-start.1
  2.1 0.7 %copy-done.1 = bf16[4,4,512]{2,1,0:T(4,128)(2,1)S(1)} copy-done((bf16[4,4,512]{2,1,0:T(4,128)(2,1)S(1)}, bf16[4,4,512]{2,1,0:T(4,128)(2,1)}, u32[]{:S(2)}) %copy-start.1) | copy-done | bytes 16408
  2.8 0.0 copy-start.2
  2.8 0.7 copy-done.2
  3.4 0.0 copy-start.3
  3.4 0.7 copy-done.3
  4.1 0.0 copy-start.4
  4.1 0.7 copy-done.4
  4.8 60.8 %shard_map.82 = bf16[64,2048]{1,0:T(8,128)(2,1)S(1)} custom-call(bf16[64,2048]{1,0:T(8,128)(2,1)S(1)} %copy-done, bf16[2048,3072]{1,0:T(8,128)(2,1)} %wp_ref.1, bf16[2048,16]{1,0:T(8,128)(2,1)S(1)} %copy.9.wm_ref, bf16[4,4,512]{2,1,0:T(4,128)(2,1)S(1)} %copy-done.1, f32[1,8]{1,0:T(1,128)S(1)} %bitcast.3, f32[1,8]{1,0:T(1,128)S(1)} %bitcast.4, ...), custom_call_target="tpu_custom_call" | custom-call | tf_op jit(solution)/shard_map/pallas_call | solution.py:321
  65.6 0.7 %copy.11 = bf16[64,2048]{1,0:T(8,128)(2,1)} copy(bf16[64,2048]{1,0:T(8,128)(2,1)S(1)} %shard_map.82) | data formatting | bytes 524288
Async XLA Ops:
  1.1 1.0 %copy-start = (bf16[64,2048]{1,0:T(8,128)(2,1)S(1)}, bf16[64,2048]{1,0:T(8,128)(2,1)}, u32[]{:S(2)}) copy-start(bf16[64,2048]{1,0:T(8,128)(2,1)} %tok_ref.1) | copy-start | bytes 786436
  2.1 0.7 %copy-start.1 = (bf16[4,4,512]{2,1,0:T(4,128)(2,1)S(1)}, bf16[4,4,512]{2,1,0:T(4,128)(2,1)}, u32[]{:S(2)}) copy-start(bf16[4,4,512]{2,1,0:T(4,128)(2,1)} %cw_ref.1) | copy-start | bytes 49156
  2.8 0.7 copy-start.2
  3.4 0.7 copy-start.3
  4.1 0.7 copy-start.4

commit v2 on v1

v2 whole, which is shorter than its diff:
```python
import functools

import jax
import jax.numpy as jnp
from jax import lax
from jax.experimental import pallas as pl
from jax.experimental.pallas import tpu as pltpu
from jax.sharding import PartitionSpec as P

EPSILON = 1e-06
TOP_PRECISION = lax.Precision.HIGHEST
MESH = pl.DeviceIdType.MESH
WIDTH = 128
F32 = jnp.float32
BF16 = jnp.bfloat16
BORDER = 16
LEAST_LOG = -120.0


def mm(a, b):
    return jnp.dot(a, b, preferred_element_type=F32)


def mm_rows(a, b):
    return lax.dot_general(a, b, (((1,), (1,)), ((), ())), preferred_element_type=F32)


def mm_over_rows(a, b):
    return lax.dot_general(a, b, (((0,), (0,)), ((), ())), preferred_element_type=F32)


def sigmoid(x):
    return 1.0 / (1.0 + jnp.exp(-x))


def softplus(x):
    small = jnp.exp(-jnp.abs(x))
    grown = 1.0 + small
    tail = jnp.where(grown == 1.0, small, jnp.log(grown) * small / jnp.where(grown == 1.0, 1.0, grown - 1.0))
    return jnp.maximum(x, 0.0) + tail


def kernel(
    n_ctx, n_tp, key_heads, batch, chunks,
    tok_ref, wp_ref, wm_ref, cw_in, dl_in, sb_in, gain_in, wo_ref,
    out_ref,
    gath, wp, wm, wo, cw_ref, dl_ref, sb_ref, gain_ref,
    ext, act, border_out, border_in, col, row, solutions, minus, inject, own, reach,
    s_in, s_out, decay_all, normed, stage, landed,
    own_sem, wp_sem, small_sem, wo_sem, ag_send, ag_recv, border_sem, state_send, state_recv, rs_send, rs_recv,
):
    rows = tok_ref.shape[0]
    length = rows * n_tp
    heads = 2 * key_heads
    depth = wo_ref.shape[1]
    ctx, tp = lax.axis_index("ctx"), lax.axis_index("tp")
    six, four = 6 * WIDTH, 4 * WIDTH

    k_rows = depth // chunks
    small_copies = [
        pltpu.make_async_copy(source, target, small_sem.at[n])
        for n, (source, target) in enumerate(
            [(wm_ref, wm), (cw_in, cw_ref), (dl_in, dl_ref), (sb_in, sb_ref), (gain_in, gain_ref)]
        )
    ]
    wo_copy = pltpu.make_async_copy(wo_ref, wo, wo_sem)
    wp_copies = [
        pltpu.make_async_copy(wp_ref.at[pl.ds(k * k_rows, k_rows)], wp.at[pl.ds(k * k_rows, k_rows)], wp_sem.at[k])
        for k in range(chunks)
    ]
    mine = pl.ds(pl.multiple_of(tp * rows, 16), rows)
    own_copy = pltpu.make_async_copy(tok_ref, gath.at[mine], own_sem)
    own_copy.start()
    for copy in wp_copies:
        copy.start()
    for copy in small_copies:
        copy.start()
    wo_copy.start()

    barrier = pltpu.get_barrier_semaphore()
    peers = [lax.rem(tp + k, n_tp) for k in range(1, n_tp)]
    for peer in peers:
        pl.semaphore_signal(barrier, inc=1, device_id={"tp": peer}, device_id_type=MESH)

    @pl.when(ctx > 0)
    def _():
        pl.semaphore_signal(barrier, inc=1, device_id={"ctx": ctx - 1}, device_id_type=MESH)

    @pl.when(ctx < n_ctx - 1)
    def _():
        pl.semaphore_signal(barrier, inc=1, device_id={"ctx": ctx + 1}, device_id_type=MESH)

    beside = jnp.where(ctx > 0, 1, 0) + jnp.where(ctx < n_ctx - 1, 1, 0)
    pl.semaphore_wait(barrier, n_tp - 1 + beside)

    def block_copy(source, held, peer, way, k):
        place = pl.ds(k * k_rows, k_rows)
        return pltpu.make_async_remote_copy(
            src_ref=source.at[:, place] if held is mine else source.at[held, place],
            dst_ref=gath.at[held, place],
            send_sem=ag_send.at[way, k], recv_sem=ag_recv.at[way, k],
            device_id={"tp": peer}, device_id_type=MESH,
        )

    def project(k):
        wp_copies[k].wait()
        place = slice(k * k_rows, (k + 1) * k_rows)

        def tile(t, carry):
            span = pl.ds(pl.multiple_of(t * 256, 256), 256)
            part = mm(gath[:, place], wp[place, span])
            if k > 0:
                part = part + ext[8 : 8 + length, span]
            if k == chunks - 1:
                part = part.astype(BF16).astype(F32)
            ext[8 : 8 + length, span] = part
            return carry

        lax.fori_loop(0, key_heads * six // 256, tile, 0)

    if n_tp == 4:
        x_peer = tp + 1 - 2 * lax.rem(tp, 2)
        y_peer = lax.rem(tp + 2, 4)
        x_rows = pl.ds(pl.multiple_of(x_peer * rows, 16), rows)
        y_rows = pl.ds(pl.multiple_of(y_peer * rows, 16), rows)
        direct = [
            [block_copy(tok_ref, mine, peer, way, k) for way, peer in enumerate((x_peer, y_peer))]
            for k in range(chunks)
        ]
        passed = [
            block_copy(gath, x_rows, y_peer, 2, k) if k % 2 == 0 else block_copy(gath, y_rows, x_peer, 2, k)
            for k in range(chunks)
        ]
        for pair in direct:
            for copy in pair:
                copy.start()
        own_copy.wait()
        for k in range(chunks):
            for copy in direct[k]:
                copy.wait_recv()
            passed[k].start()
            if k > 0:
                passed[k - 1].wait_recv()
                project(k - 1)
        passed[chunks - 1].wait_recv()
        project(chunks - 1)
        sent = [copy for pair in direct for copy in pair] + passed
    else:
        sent = [block_copy(tok_ref, mine, peer, way, k) for k in range(chunks) for way, peer in enumerate(peers)]
        for copy in sent:
            copy.start()
        own_copy.wait()
        for k in range(chunks):
            for way in range(n_tp - 1):
                sent[k * (n_tp - 1) + way].wait_recv()
            project(k)

    for g in range(key_heads):
        border_out[:, g * four : (g + 1) * four] = ext[
            8 + length - BORDER : 8 + length, g * six : g * six + four
        ].astype(BF16)
    border_copy = pltpu.make_async_remote_copy(
        src_ref=border_out, dst_ref=border_in, send_sem=border_sem.at[0], recv_sem=border_sem.at[1],
        device_id={"ctx": lax.rem(ctx + 1, n_ctx)}, device_id_type=MESH,
    )

    @pl.when(ctx < n_ctx - 1)
    def _():
        border_copy.start()

    for copy in small_copies:
        copy.wait()
    mixers = mm_rows(gath[...], wm[...]).astype(BF16).astype(F32)
    columns = mixers.shape[1]
    lane = lax.broadcasted_iota(jnp.int32, (1, columns), 1)
    rate = jnp.zeros((1, columns), F32)
    bias = jnp.zeros((1, columns), F32)
    for h in range(heads):
        here = lane == 4 * (h // 2) + 2 + h % 2
        rate = jnp.where(here, dl_ref[h], rate)
        bias = jnp.where(here, sb_ref[h], bias)
    strength = sigmoid(mixers)
    log_decay = jnp.maximum(-jnp.exp(rate) * softplus(mixers + bias), LEAST_LOG)
    at_row = lax.broadcasted_iota(jnp.int32, (length, length), 0)
    at_col = lax.broadcasted_iota(jnp.int32, (length, length), 1)
    lower = jnp.where(at_row >= at_col, 1.0, 0.0)
    cumulative = jnp.dot(lower, log_decay, precision=TOP_PRECISION, preferred_element_type=F32)

    ext[0:8, :] = jnp.zeros((8, ext.shape[1]), F32)

    def convolve(count):
        def one(g, carry):
            for t in range(4):
                place = pl.ds(pl.multiple_of(g * six + t * WIDTH, WIDTH), WIDTH)
                taps = cw_ref[g, :, t * WIDTH : (t + 1) * WIDTH].astype(F32)
                total = taps[0:1] * ext[5 : 5 + count, place]
                for j in range(1, 4):
                    total = total + taps[j : j + 1] * ext[5 + j : 5 + j + count, place]
                target = pl.ds(pl.multiple_of(g * four + t * WIDTH, WIDTH), WIDTH)
                act[0:count, target] = (total * sigmoid(total)).astype(BF16)
            return carry

        lax.fori_loop(0, key_heads, one, 0)

    convolve(length)

    @pl.when(ctx > 0)
    def _():
        border_copy.wait_recv()
        for g in range(key_heads):
            ext[0:8, g * six : g * six + four] = border_in[BORDER - 8 : BORDER, g * four : (g + 1) * four].astype(F32)
        convolve(BORDER)

    wide = lax.broadcasted_iota(jnp.int32, (length, WIDTH), 1)
    for g in range(key_heads):
        query = act[:, g * four : g * four + WIDTH].astype(F32)
        key = act[:, g * four + WIDTH : g * four + 2 * WIDTH].astype(F32)
        query_unit = lax.rsqrt(jnp.sum(query * query, axis=1, keepdims=True) + EPSILON)
        key_unit = lax.rsqrt(jnp.sum(key * key, axis=1, keepdims=True) + EPSILON)
        for r in range(2):
            h = 2 * g + r
            cum = cumulative[:, 4 * g + 2 + r : 4 * g + 3 + r]
            beta = strength[:, 4 * g + r : 4 * g + r + 1]
            packed = jnp.where(
                wide == 0, cum, jnp.where(wide == 1, beta, jnp.where(wide == 2, key_unit, query_unit))
            )
            col[h] = packed
            row[h] = jnp.transpose(packed)[0:8]

    def heads_of(step, carry):
        i = lax.broadcasted_iota(jnp.int32, (length, length), 0)
        j = lax.broadcasted_iota(jnp.int32, (length, length), 1)
        apart = jnp.bitwise_xor(i, j)
        lows, inverses = [], []
        for b in range(batch):
            g = step * batch + b
            key = act[:, pl.ds(pl.multiple_of(g * four + WIDTH, WIDTH), WIDTH)]
            key_key = mm_rows(key, key)
            for r in range(2):
                h = 2 * g + r
                scal, across = col[h], row[h]
                cum, beta, key_unit = (scal[:, n : n + 1] for n in range(3))
                within = jnp.where(i >= j, jnp.exp(jnp.where(i >= j, cum - across[0:1], 0.0)), 0.0) * across[2:3]
                low = jnp.where(i > j, within * key_key * (beta * key_unit), 0.0).astype(BF16)
                lows.append(low)
                inverses.append(jnp.where(i == j, 1.0, jnp.where(apart == 1, -low.astype(F32), 0.0)).astype(BF16))
        span = 2
        while span < length:
            between = (apart >= span) & (apart < 2 * span)
            firsts = [
                mm(t, jnp.where(between, low.astype(F32), 0.0).astype(BF16)).astype(BF16)
                for t, low in zip(inverses, lows)
            ]
            inverses = [t - mm(first, t).astype(BF16) for t, first in zip(inverses, firsts)]
            span *= 2
        for n, inverse in enumerate(inverses):
            g = step * batch + n // 2
            r = n % 2
            h = 2 * g + r
            scal = col[h]
            cum, beta, key_unit = (scal[:, m : m + 1] for m in range(3))
            key = act[:, pl.ds(pl.multiple_of(g * four + WIDTH, WIDTH), WIDTH)].astype(F32)
            vector = act[:, pl.ds(pl.multiple_of(g * four + (2 + r) * WIDTH, WIDTH), WIDTH)].astype(F32)
            last = cum[length - 1 : length]
            right = jnp.concatenate([vector * beta, key * (beta * jnp.exp(cum) * key_unit)], axis=1).astype(BF16)
            solved = mm(inverse, right).astype(BF16)
            solutions[h] = solved
            tail = (key * (jnp.exp(last - cum) * key_unit)).astype(BF16)
            ends = mm_over_rows(tail, solved)
            inject[h] = ends[:, :WIDTH]
            minus[h] = ends[:, WIDTH:].astype(BF16)
            decay_all[h] = jnp.broadcast_to(jnp.exp(last), (8, WIDTH))
        return carry

    lax.fori_loop(0, key_heads // batch, heads_of, 0)

    def state_copy(h):
        return pltpu.make_async_remote_copy(
            src_ref=s_out.at[h], dst_ref=s_in.at[h], send_sem=state_send.at[h], recv_sem=state_recv.at[h],
            device_id={"ctx": lax.rem(ctx + 1, n_ctx)}, device_id_type=MESH,
        )

    def within_block(g, carry):
        i = lax.broadcasted_iota(jnp.int32, (length, length), 0)
        j = lax.broadcasted_iota(jnp.int32, (length, length), 1)
        query = act[:, pl.ds(pl.multiple_of(g * four, WIDTH), WIDTH)]
        key = act[:, pl.ds(pl.multiple_of(g * four + WIDTH, WIDTH), WIDTH)]
        query_key = mm_rows(query, key)
        for r in range(2):
            h = 2 * g + r
            scal, across = col[h], row[h]
            cum, query_unit = scal[:, 0:1], scal[:, 3:4]
            within = jnp.where(i >= j, jnp.exp(jnp.where(i >= j, cum - across[0:1], 0.0)), 0.0) * across[2:3]
            local = mm((within * query_key * query_unit).astype(BF16), solutions[h])
            own[h] = local[:, :WIDTH]
            reach[h] = (query.astype(F32) * (jnp.exp(cum) * query_unit) - local[:, WIDTH:]).astype(BF16)
        return carry

    def finish(h):
        core = (own[h] + mm(reach[h], s_in[h])).astype(BF16).astype(F32)
        gated = ext[8 : 8 + length, pl.ds(pl.multiple_of((h // 2) * six + four + (h % 2) * WIDTH, WIDTH), WIDTH)]
        scaled = core * lax.rsqrt(jnp.mean(core * core, axis=1, keepdims=True) + EPSILON)
        normed[:, pl.ds(pl.multiple_of(h * WIDTH, WIDTH), WIDTH)] = (
            gain_ref[...] * scaled * (gated * sigmoid(gated))
        ).astype(BF16)

    early = ctx < n_ctx // 2 - 1

    @pl.when(jnp.logical_not(early))
    def _():
        lax.fori_loop(0, key_heads, within_block, 0)

    for h in range(heads):
        @pl.when(ctx > 0)
        def _():
            state_copy(h).wait_recv()

        @pl.when(ctx == 0)
        def _():
            s_in[h] = jnp.zeros((WIDTH, WIDTH), BF16)

        @pl.when(ctx < n_ctx - 1)
        def _():
            before = s_in[h]
            after = decay_all[h, 0:1, :] * before.astype(F32) - mm(minus[h], before) + inject[h]
            s_out[h] = after.astype(BF16)
            state_copy(h).start()

        @pl.when(ctx == n_ctx - 1)
        def _():
            finish(h)

    @pl.when(early)
    def _():
        lax.fori_loop(0, key_heads, within_block, 0)

    @pl.when(ctx < n_ctx - 1)
    def _():
        def one(h, carry):
            finish(h)
            return carry

        lax.fori_loop(0, heads, one, 0)

    wo_copy.wait()
    pieces = rs_send.shape[0]
    piece = depth // pieces

    def share_copy(q, k):
        peer = lax.rem(tp + k + 1, n_tp)
        place = pl.ds(q * piece, piece)
        return pltpu.make_async_remote_copy(
            src_ref=stage.at[pl.ds(pl.multiple_of(peer * rows, 16), rows), place],
            dst_ref=landed.at[k, :, place],
            send_sem=rs_send.at[q, k], recv_sem=rs_recv.at[q, k],
            device_id={"tp": peer}, device_id_type=MESH,
        )

    for q in range(pieces):
        for t in range(0, piece, 256):
            place = slice(q * piece + t, q * piece + t + 256)
            stage[:, place] = mm(normed[...], wo[:, place]).astype(BF16)
        for k in range(n_tp - 1):
            share_copy(q, k).start()
    for q in range(pieces):
        place = slice(q * piece, (q + 1) * piece)
        total = stage[mine, place].astype(F32)
        for k in range(n_tp - 1):
            share_copy(q, k).wait_recv()
            total = total + landed[k, :, place].astype(F32)
        out_ref[:, place] = total.astype(BF16)
    for q in range(pieces):
        for k in range(n_tp - 1):
            share_copy(q, k).wait_send()
    for copy in sent:
        copy.wait_send()

    @pl.when(ctx < n_ctx - 1)
    def _():
        border_copy.wait_send()
        for h in range(heads):
            state_copy(h).wait_send()


def on_device(tokens, w_project, w_mixers, conv_weight, decay_log, step_bias, norm_gain, w_output):
    n_ctx, n_tp = lax.axis_size("ctx"), lax.axis_size("tp")
    rows, depth = tokens.shape
    length = rows * n_tp
    key_heads = conv_weight.shape[0]
    heads = 2 * key_heads
    inner = heads * WIDTH
    batch = 2 if key_heads % 2 == 0 else 1
    pieces = 4
    chunks = 4
    ways = 3 if n_tp == 4 else n_tp - 1
    vmem = pl.BlockSpec(memory_space=pltpu.VMEM)
    far = pl.BlockSpec(memory_space=pl.ANY)
    dma = pltpu.SemaphoreType.DMA
    square = (heads, WIDTH, WIDTH)
    return pl.pallas_call(
        functools.partial(kernel, n_ctx, n_tp, key_heads, batch, chunks),
        out_shape=jax.ShapeDtypeStruct((rows, depth), BF16),
        in_specs=[far] * 8,
        out_specs=vmem,
        scratch_shapes=[
            pltpu.VMEM((length, depth), BF16),
            pltpu.VMEM(w_project.shape, BF16),
            pltpu.VMEM((w_mixers.shape[1], depth), BF16),
            pltpu.VMEM(w_output.shape, BF16),
            pltpu.VMEM(conv_weight.shape, BF16),
            pltpu.SMEM((heads,), F32),
            pltpu.SMEM((heads,), F32),
            pltpu.VMEM((1, WIDTH), F32),
            pltpu.VMEM((8 + length, key_heads * 6 * WIDTH), F32),
            pltpu.VMEM((length, key_heads * 4 * WIDTH), BF16),
            pltpu.VMEM((BORDER, key_heads * 4 * WIDTH), BF16),
            pltpu.VMEM((BORDER, key_heads * 4 * WIDTH), BF16),
            pltpu.VMEM((heads, length, WIDTH), F32),
            pltpu.VMEM((heads, 8, length), F32),
            pltpu.VMEM((heads, length, 2 * WIDTH), BF16),
            pltpu.VMEM(square, BF16),
            pltpu.VMEM(square, F32),
            pltpu.VMEM((heads, length, WIDTH), F32),
            pltpu.VMEM((heads, length, WIDTH), BF16),
            pltpu.VMEM(square, BF16),
            pltpu.VMEM(square, BF16),
            pltpu.VMEM((heads, 8, WIDTH), F32),
            pltpu.VMEM((length, inner), BF16),
            pltpu.VMEM((length, depth), BF16),
            pltpu.VMEM((n_tp - 1, rows, depth), BF16),
            dma, dma((chunks,)), dma((5,)), dma,
            dma((ways, chunks)), dma((ways, chunks)), dma((2,)),
            dma((heads,)), dma((heads,)),
            dma((pieces, n_tp - 1)), dma((pieces, n_tp - 1)),
        ],
        compiler_params=pltpu.CompilerParams(
            collective_id=0, has_side_effects=True, vmem_limit_bytes=63 * 1024 * 1024
        ),
    )(
        tokens, w_project, w_mixers.T, conv_weight, decay_log, step_bias, norm_gain.reshape(1, WIDTH), w_output,
    )


def solution(mesh):
    placed = (
        P(("ctx", "tp"), None),
        P(None, "tp"),
        P(None, "tp"),
        P("tp", None, None),
        P("tp"),
        P("tp"),
        P(),
        P("tp", None),
    )
    return jax.shard_map(
        on_device, mesh=mesh, in_specs=placed, out_specs=P(("ctx", "tp"), None), check_vma=False
    )
```

time: 67.2 us -> 65.1 us (0.969); the launches traced: 66.3 us -> 65 us
  local copies, waits for them, and re-layouts: 5.44 us -> 1.67 us
  Pallas kernels: 60.8 us -> 63.3 us
    unnamed x12 -> x1, local copies, waits for them, and re-layouts: 5.44 us -> 1.67 us
    pallas_call x1, Pallas kernels: 60.8 us -> 63.3 us  [on_device(): pl.pallas_call(functools.partial(kernel, n_ctx, n_tp, key_heads, batch, c...]
where the time goes in v2:
time: 65.1 us; the launch traced here: 65 us
  Pallas kernels  63.3 us (97%)
  local copies, waits for them, and re-layouts  1.67 us (3%)
    pallas_call x1, Pallas kernels, on_device(): pl.pallas_call(functools.partial(kernel, n_ctx, n_tp, key_heads, batch, c...  63.3 us
    unnamed x1, local copies, waits for them, and re-layouts  1.67 us

profile of v2, /device:TPU:24, one launch (start us, length us, event | category | flops | bytes accessed | tf_op | source)
XLA Modules:
  0.0 65.0 jit_solution(16602559704538179424)
XLA Ops:
  0.0 63.3 %shard_map.82 = bf16[64,2048]{1,0:T(8,128)(2,1)} custom-call(bf16[64,2048]{1,0:T(8,128)(2,1)} %tok_ref.1, bf16[2048,3072]{1,0:T(8,128)(2,1)} %wp_ref.1, bf16[16,2048]{1,0:T(8,128)(2,1)} %bitcast.2, bf16[4,4,512]{2,1,0:T(4,128)(2,1)} %cw_in.1, f32[8]{0:T(128)} %dl_in.1, f32[8]{0:T(128)} %sb_in.1, f32[1,128]{1,0:T(1,128)} %bitcast.3, bf16[1024,2048]{1,0:T(8,128)(2,1)} %wo_ref.1), custom_call_target="tpu_custom_call" | custom-call | tf_op jit(solution)/shard_map/pallas_call | solution.py:400
  63.3 1.7 %copy.10 = bf16[64,2048]{1,0:T(8,128)(2,1)} copy(bf16[64,2048]{1,0:T(8,128)(2,1)} %shard_map.82) | data formatting | bytes 524288

commit v3 on v2

--- a/solution.py
+++ b/solution.py
@@ -71,11 +71,8 @@
     mine = pl.ds(pl.multiple_of(tp * rows, 16), rows)
     own_copy = pltpu.make_async_copy(tok_ref, gath.at[mine], own_sem)
     own_copy.start()
-    for copy in wp_copies:
+    for copy in wp_copies[: chunks // 2]:
         copy.start()
-    for copy in small_copies:
-        copy.start()
-    wo_copy.start()
 
     barrier = pltpu.get_barrier_semaphore()
     peers = [lax.rem(tp + k, n_tp) for k in range(1, n_tp)]
@@ -102,21 +99,25 @@
             device_id={"tp": peer}, device_id_type=MESH,
         )
 
-    def project(k):
-        wp_copies[k].wait()
-        place = slice(k * k_rows, (k + 1) * k_rows)
-
-        def tile(t, carry):
-            span = pl.ds(pl.multiple_of(t * 256, 256), 256)
+    def project(half):
+        groups = chunks // 2
+        for k in range(half * groups, (half + 1) * groups):
+            wp_copies[k].wait()
+        place = slice(half * groups * k_rows, (half + 1) * groups * k_rows)
+        total_columns = key_heads * six
+        for start in range(0, total_columns, 256):
+            span = slice(start, start + 256)
             part = mm(gath[:, place], wp[place, span])
-            if k > 0:
-                part = part + ext[8 : 8 + length, span]
-            if k == chunks - 1:
-                part = part.astype(BF16).astype(F32)
+            if half == 1:
+                part = (part + ext[8 : 8 + length, span]).astype(BF16).astype(F32)
             ext[8 : 8 + length, span] = part
-            return carry
-
-        lax.fori_loop(0, key_heads * six // 256, tile, 0)
+
+    def start_rest():
+        for copy in wp_copies[chunks // 2 :]:
+            copy.start()
+        for copy in small_copies:
+            copy.start()
+        wo_copy.start()
 
     if n_tp == 4:
         x_peer = tp + 1 - 2 * lax.rem(tp, 2)
@@ -134,26 +135,31 @@
         for pair in direct:
             for copy in pair:
                 copy.start()
+        start_rest()
         own_copy.wait()
         for k in range(chunks):
             for copy in direct[k]:
                 copy.wait_recv()
             passed[k].start()
-            if k > 0:
-                passed[k - 1].wait_recv()
-                project(k - 1)
-        passed[chunks - 1].wait_recv()
-        project(chunks - 1)
+            if k == chunks - 1:
+                for early_copy in passed[: chunks // 2]:
+                    early_copy.wait_recv()
+                project(0)
+        for late_copy in passed[chunks // 2 :]:
+            late_copy.wait_recv()
+        project(1)
         sent = [copy for pair in direct for copy in pair] + passed
     else:
         sent = [block_copy(tok_ref, mine, peer, way, k) for k in range(chunks) for way, peer in enumerate(peers)]
         for copy in sent:
             copy.start()
+        start_rest()
         own_copy.wait()
         for k in range(chunks):
             for way in range(n_tp - 1):
                 sent[k * (n_tp - 1) + way].wait_recv()
-            project(k)
+            if (k + 1) % (chunks // 2) == 0:
+                project((k + 1) // (chunks // 2) - 1)
 
     for g in range(key_heads):
         border_out[:, g * four : (g + 1) * four] = ext[
@@ -389,12 +395,12 @@
     key_heads = conv_weight.shape[0]
     heads = 2 * key_heads
     inner = heads * WIDTH
-    batch = 2 if key_heads % 2 == 0 else 1
+    batch = next(n for n in (4, 2, 1) if key_heads % n == 0)
     pieces = 4
     chunks = 4
     ways = 3 if n_tp == 4 else n_tp - 1
     vmem = pl.BlockSpec(memory_space=pltpu.VMEM)
-    far = pl.BlockSpec(memory_space=pl.ANY)
+    far = pl.BlockSpec(memory_space=pltpu.HBM)
     dma = pltpu.SemaphoreType.DMA
     square = (heads, WIDTH, WIDTH)
     return pl.pallas_call(
@@ -434,7 +440,7 @@
             dma((pieces, n_tp - 1)), dma((pieces, n_tp - 1)),
         ],
         compiler_params=pltpu.CompilerParams(
-            collective_id=0, has_side_effects=True, vmem_limit_bytes=63 * 1024 * 1024
+            collective_id=0, has_side_effects=True, vmem_limit_bytes=52 * 1024 * 1024
         ),
     )(
         tokens, w_project, w_mixers.T, conv_weight, decay_log, step_bias, norm_gain.reshape(1, WIDTH), w_output,

time: 65.1 us -> 61.3 us (0.942)
  Pallas kernels: 63.3 us -> 55.8 us
  local copies, waits for them, and re-layouts: 1.67 us -> 5.17 us
    pallas_call x1, Pallas kernels: 63.3 us -> 55.8 us  [on_device(): pl.pallas_call(functools.partial(kernel, n_ctx, n_tp, key_heads, batch, c...]
    unnamed x1 -> x13, local copies, waits for them, and re-layouts: 1.67 us -> 5.17 us
where the time goes in v3:
time: 61.3 us; the launch traced here: 61 us
  Pallas kernels  55.8 us (91%)
  local copies, waits for them, and re-layouts  5.17 us (8%)
    pallas_call x1, Pallas kernels, on_device(): pl.pallas_call(functools.partial(kernel, n_ctx, n_tp, key_heads, batch, c...  55.8 us
    unnamed x13, local copies, waits for them, and re-layouts  5.17 us

profile of v3, /device:TPU:24, one launch (start us, length us, event | category | flops | bytes accessed | tf_op | source)
XLA Modules:
  0.0 61.0 jit_solution(6256022811845418361)
XLA Ops:
  0.0 0.0 copy-start
  0.0 0.9 %copy-done = bf16[64,2048]{1,0:T(8,128)(2,1)S(1)} copy-done((bf16[64,2048]{1,0:T(8,128)(2,1)S(1)}, bf16[64,2048]{1,0:T(8,128)(2,1)}, u32[]{:S(2)}) %copy-start) | copy-done | bytes 262168
  1.0 0.0 copy-start.1
  1.0 0.8 %copy-done.1 = bf16[2048,16]{0,1:T(8,128)(2,1)S(1)} copy-done((bf16[2048,16]{0,1:T(8,128)(2,1)S(1)}, bf16[2048,16]{0,1:T(8,128)(2,1)}, u32[]{:S(2)}) %copy-start.1) | copy-done | bytes 65560
  1.8 0.0 copy-start.2
  1.8 0.7 %copy-done.2 = bf16[4,4,512]{2,1,0:T(4,128)(2,1)S(1)} copy-done((bf16[4,4,512]{2,1,0:T(4,128)(2,1)S(1)}, bf16[4,4,512]{2,1,0:T(4,128)(2,1)}, u32[]{:S(2)}) %copy-start.2) | copy-done | bytes 16408
  2.5 0.0 copy-start.3
  2.5 0.7 %copy-done.3 = f32[8]{0:T(128)S(1)} copy-done((f32[8]{0:T(128)S(1)}, f32[8]{0:T(128)}, u32[]{:S(2)}) %copy-start.3) | copy-done | bytes 56
  3.2 0.0 copy-start.4
  3.2 0.7 %copy-done.4 = f32[8]{0:T(128)S(1)} copy-done((f32[8]{0:T(128)S(1)}, f32[8]{0:T(128)}, u32[]{:S(2)}) %copy-start.4) | copy-done | bytes 56
  3.8 0.0 copy-start.5
  3.8 0.7 %copy-done.5 = f32[128]{0:T(128)S(1)} copy-done((f32[128]{0:T(128)S(1)}, f32[128]{0:T(128)}, u32[]{:S(2)}) %copy-start.5) | copy-done | bytes 536
  4.5 55.8 %shard_map.82 = bf16[64,2048]{1,0:T(8,128)(2,1)S(1)} custom-call(bf16[64,2048]{1,0:T(8,128)(2,1)S(1)} %copy-done, bf16[2048,3072]{1,0:T(8,128)(2,1)} %wp_ref.1, bf16[16,2048]{1,0:T(8,128)(2,1)S(1)} %bitcast.2, bf16[4,4,512]{2,1,0:T(4,128)(2,1)S(1)} %copy-done.2, f32[8]{0:T(128)S(1)} %copy-done.3, f32[8]{0:T(128)S(1)} %copy-done.4, f32[1,128]{1,0:T(1,128)S(1)} %bitcast.3, ...), custom_call_target="tpu_custom_call" | custom-call | tf_op jit(solution)/shard_map/pallas_call | solution.py:406
  60.3 0.7 %copy.10 = bf16[64,2048]{1,0:T(8,128)(2,1)} copy(bf16[64,2048]{1,0:T(8,128)(2,1)S(1)} %shard_map.82) | data formatting | bytes 524288
Async XLA Ops:
  0.0 0.9 %copy-start = (bf16[64,2048]{1,0:T(8,128)(2,1)S(1)}, bf16[64,2048]{1,0:T(8,128)(2,1)}, u32[]{:S(2)}) copy-start(bf16[64,2048]{1,0:T(8,128)(2,1)} %tok_ref.1) | copy-start | bytes 786436
  1.0 0.8 %copy-start.1 = (bf16[2048,16]{0,1:T(8,128)(2,1)S(1)}, bf16[2048,16]{0,1:T(8,128)(2,1)}, u32[]{:S(2)}) copy-start(bf16[2048,16]{0,1:T(8,128)(2,1)} %param.10) | copy-start | bytes 196612
  1.8 0.7 %copy-start.2 = (bf16[4,4,512]{2,1,0:T(4,128)(2,1)S(1)}, bf16[4,4,512]{2,1,0:T(4,128)(2,1)}, u32[]{:S(2)}) copy-start(bf16[4,4,512]{2,1,0:T(4,128)(2,1)} %cw_in.1) | copy-start | bytes 49156
  2.5 0.7 %copy-start.3 = (f32[8]{0:T(128)S(1)}, f32[8]{0:T(128)}, u32[]{:S(2)}) copy-start(f32[8]{0:T(128)} %dl_in.1) | copy-start | bytes 100
  3.2 0.7 %copy-start.4 = (f32[8]{0:T(128)S(1)}, f32[8]{0:T(128)}, u32[]{:S(2)}) copy-start(f32[8]{0:T(128)} %sb_in.1) | copy-start | bytes 100
  3.8 0.7 %copy-start.5 = (f32[128]{0:T(128)S(1)}, f32[128]{0:T(128)}, u32[]{:S(2)}) copy-start(f32[128]{0:T(128)} %param.14) | copy-start | bytes 1540

commit v4 on v3

--- a/solution.py
+++ b/solution.py
@@ -246,17 +246,14 @@
                 h = 2 * g + r
                 scal, across = col[h], row[h]
                 cum, beta, key_unit = (scal[:, n : n + 1] for n in range(3))
-                within = jnp.where(i >= j, jnp.exp(jnp.where(i >= j, cum - across[0:1], 0.0)), 0.0) * across[2:3]
+                within = jnp.exp(jnp.where(i > j, cum - across[0:1], 0.0)) * across[2:3]
                 low = jnp.where(i > j, within * key_key * (beta * key_unit), 0.0).astype(BF16)
                 lows.append(low)
                 inverses.append(jnp.where(i == j, 1.0, jnp.where(apart == 1, -low.astype(F32), 0.0)).astype(BF16))
         span = 2
         while span < length:
-            between = (apart >= span) & (apart < 2 * span)
-            firsts = [
-                mm(t, jnp.where(between, low.astype(F32), 0.0).astype(BF16)).astype(BF16)
-                for t, low in zip(inverses, lows)
-            ]
+            between = jnp.where((apart >= span) & (apart < 2 * span), 1.0, 0.0).astype(BF16)
+            firsts = [mm(t, low * between).astype(BF16) for t, low in zip(inverses, lows)]
             inverses = [t - mm(first, t).astype(BF16) for t, first in zip(inverses, firsts)]
             span *= 2
         for n, inverse in enumerate(inverses):
@@ -286,6 +283,9 @@
             device_id={"ctx": lax.rem(ctx + 1, n_ctx)}, device_id_type=MESH,
         )
 
+    def gate_place(h):
+        return pl.ds(pl.multiple_of((h // 2) * six + four + (h % 2) * WIDTH, WIDTH), WIDTH)
+
     def within_block(g, carry):
         i = lax.broadcasted_iota(jnp.int32, (length, length), 0)
         j = lax.broadcasted_iota(jnp.int32, (length, length), 1)
@@ -300,14 +300,16 @@
             local = mm((within * query_key * query_unit).astype(BF16), solutions[h])
             own[h] = local[:, :WIDTH]
             reach[h] = (query.astype(F32) * (jnp.exp(cum) * query_unit) - local[:, WIDTH:]).astype(BF16)
+            gated = ext[8 : 8 + length, gate_place(h)]
+            ext[8 : 8 + length, gate_place(h)] = gain_ref[...] * (gated * sigmoid(gated))
         return carry
 
     def finish(h):
         core = (own[h] + mm(reach[h], s_in[h])).astype(BF16).astype(F32)
-        gated = ext[8 : 8 + length, pl.ds(pl.multiple_of((h // 2) * six + four + (h % 2) * WIDTH, WIDTH), WIDTH)]
+        gated = ext[8 : 8 + length, gate_place(h)]
         scaled = core * lax.rsqrt(jnp.mean(core * core, axis=1, keepdims=True) + EPSILON)
         normed[:, pl.ds(pl.multiple_of(h * WIDTH, WIDTH), WIDTH)] = (
-            gain_ref[...] * scaled * (gated * sigmoid(gated))
+            scaled * gated
         ).astype(BF16)
 
     early = ctx < n_ctx // 2 - 1
@@ -400,7 +402,7 @@
     chunks = 4
     ways = 3 if n_tp == 4 else n_tp - 1
     vmem = pl.BlockSpec(memory_space=pltpu.VMEM)
-    far = pl.BlockSpec(memory_space=pltpu.HBM)
+    far = pl.BlockSpec(memory_space=pl.ANY)
     dma = pltpu.SemaphoreType.DMA
     square = (heads, WIDTH, WIDTH)
     return pl.pallas_call(
@@ -440,7 +442,7 @@
             dma((pieces, n_tp - 1)), dma((pieces, n_tp - 1)),
         ],
         compiler_params=pltpu.CompilerParams(
-            collective_id=0, has_side_effects=True, vmem_limit_bytes=52 * 1024 * 1024
+            collective_id=0, has_side_effects=True, vmem_limit_bytes=63 * 1024 * 1024
         ),
     )(
         tokens, w_project, w_mixers.T, conv_weight, decay_log, step_bias, norm_gain.reshape(1, WIDTH), w_output,

time: 61.3 us -> 58.8 us (0.959)
  local copies, waits for them, and re-layouts: 5.17 us -> 1.67 us
  Pallas kernels: 55.8 us -> 56.9 us
    unnamed x13 -> x1, local copies, waits for them, and re-layouts: 5.17 us -> 1.67 us
    pallas_call x1, Pallas kernels: 55.8 us -> 56.9 us  [on_device(): pl.pallas_call(functools.partial(kernel, n_ctx, n_tp, key_heads, batch, c...]
where the time goes in v4:
time: 58.8 us; the launch traced here: 58.6 us
  Pallas kernels  56.9 us (97%)
  local copies, waits for them, and re-layouts  1.67 us (3%)
    pallas_call x1, Pallas kernels, on_device(): pl.pallas_call(functools.partial(kernel, n_ctx, n_tp, key_heads, batch, c...  56.9 us
    unnamed x1, local copies, waits for them, and re-layouts  1.67 us

profile of v4, /device:TPU:24, one launch (start us, length us, event | category | flops | bytes accessed | tf_op | source)
XLA Modules:
  0.0 58.6 jit_solution(3420432690942745094)
XLA Ops:
  0.0 56.9 %shard_map.82 = bf16[64,2048]{1,0:T(8,128)(2,1)} custom-call(bf16[64,2048]{1,0:T(8,128)(2,1)} %tok_ref.1, bf16[2048,3072]{1,0:T(8,128)(2,1)} %wp_ref.1, bf16[16,2048]{1,0:T(8,128)(2,1)} %bitcast.2, bf16[4,4,512]{2,1,0:T(4,128)(2,1)} %cw_in.1, f32[8]{0:T(128)} %dl_in.1, f32[8]{0:T(128)} %sb_in.1, f32[1,128]{1,0:T(1,128)} %bitcast.3, bf16[1024,2048]{1,0:T(8,128)(2,1)} %wo_ref.1), custom_call_target="tpu_custom_call" | custom-call | tf_op jit(solution)/shard_map/pallas_call | solution.py:408
  56.9 1.7 %copy.10 = bf16[64,2048]{1,0:T(8,128)(2,1)} copy(bf16[64,2048]{1,0:T(8,128)(2,1)} %shard_map.82) | data formatting | bytes 524288

commit v5 on v4

--- a/solution.py
+++ b/solution.py
@@ -344,11 +344,8 @@
 
     @pl.when(ctx < n_ctx - 1)
     def _():
-        def one(h, carry):
+        for h in range(heads):
             finish(h)
-            return carry
-
-        lax.fori_loop(0, heads, one, 0)
 
     wo_copy.wait()
     pieces = rs_send.shape[0]

time: 58.8 us -> 58.3 us (level)
  Pallas kernels: 56.9 us -> 56.2 us
    pallas_call x1, Pallas kernels: 56.9 us -> 56.2 us  [on_device(): pl.pallas_call(functools.partial(kernel, n_ctx, n_tp, key_heads, batch, c...]
where the time goes in v5:
time: 58.3 us; the launch traced here: 57.9 us
  Pallas kernels  56.2 us (96%)
  local copies, waits for them, and re-layouts  1.67 us (3%)
    pallas_call x1, Pallas kernels, on_device(): pl.pallas_call(functools.partial(kernel, n_ctx, n_tp, key_heads, batch, c...  56.2 us
    unnamed x1, local copies, waits for them, and re-layouts  1.67 us

profile of v5, /device:TPU:24, one launch (start us, length us, event | category | flops | bytes accessed | tf_op | source)
XLA Modules:
  0.0 57.9 jit_solution(8445146026042345793)
XLA Ops:
  0.0 56.2 %shard_map.82 = bf16[64,2048]{1,0:T(8,128)(2,1)} custom-call(bf16[64,2048]{1,0:T(8,128)(2,1)} %tok_ref.1, bf16[2048,3072]{1,0:T(8,128)(2,1)} %wp_ref.1, bf16[16,2048]{1,0:T(8,128)(2,1)} %bitcast.2, bf16[4,4,512]{2,1,0:T(4,128)(2,1)} %cw_in.1, f32[8]{0:T(128)} %dl_in.1, f32[8]{0:T(128)} %sb_in.1, f32[1,128]{1,0:T(1,128)} %bitcast.3, bf16[1024,2048]{1,0:T(8,128)(2,1)} %wo_ref.1), custom_call_target="tpu_custom_call" | custom-call | tf_op jit(solution)/shard_map/pallas_call | solution.py:405
  56.2 1.7 %copy.10 = bf16[64,2048]{1,0:T(8,128)(2,1)} copy(bf16[64,2048]{1,0:T(8,128)(2,1)} %shard_map.82) | data formatting | bytes 524288
